TPU v7x, 32 devices: a whole 2x2x4 slice. The times are simulated.
32 devices in a mesh: seq: 32 (over z, y, x, core).
Axes of the slice: x: 2, y: 2, z: 4, core: 2. Of those that a mesh axis runs over, the one named last changes fastest.
Arguments:
- signal: bfloat16 [32768, 512], P('seq'), may hold values from -6 to 6
- grad_out: bfloat16 [32768, 512], P('seq'), may hold values from -6 to 6
- conv_weight: bfloat16 [1024, 1024], replicated, may hold values from -0.1875 to 0.1875
- proj_weight: bfloat16 [512, 512], replicated, may hold values from -0.25 to 0.25
Outputs:
- saliency: float32 [32768, 512], P('seq')
All inputs are finite; a program needn't handle non-finite values.
Results may differ from a plain program's by a relative error of at most 0.0013.
Values may be sent and summed in bfloat16 or wider, within the bound.
A program may use at most 64 MiB of HBM per device.

v0:
```python
import jax
import jax.numpy as jnp
from jax import lax
from jax.sharding import PartitionSpec as P


def from_behind(block, axis, distance):
    devices = range(lax.axis_size(axis))
    route = [(i - distance, i) for i in devices if i - distance in devices]
    return lax.ppermute(block, axis, route)


def contract_rows(left, right):
    return lax.dot_general(
        left, right, (((1,), (1,)), ((), ())), preferred_element_type=jnp.float32
    )


def shards(signal, grad_out, conv_weight, proj_weight):
    width = signal.shape[1]
    w_past = conv_weight[:width]
    w_now = conv_weight[width:]
    past = from_behind(signal, "seq", 2)
    gates = jnp.dot(signal, w_now, preferred_element_type=jnp.float32) + jnp.dot(
        past, w_past, preferred_element_type=jnp.float32
    )
    tanh_part = jnp.tanh(gates[:, :width])
    sig_part = jax.nn.sigmoid(gates[:, width:])
    d_mixed = contract_rows(grad_out, proj_weight)
    d_tanh = d_mixed * sig_part * (1.0 - tanh_part * tanh_part)
    d_sig = d_mixed * tanh_part * sig_part * (1.0 - sig_part)
    d_gates = jnp.concatenate([d_tanh, d_sig], 1).astype(jnp.bfloat16)
    far = contract_rows(d_gates, w_past).astype(jnp.bfloat16)
    back = from_behind(far, "seq", -2).astype(jnp.float32)
    near = contract_rows(d_gates, w_now)
    return grad_out.astype(jnp.float32) + near + back


def solution(mesh):
    in_specs = (P("seq", None), P("seq", None), P(), P())
    out_specs = P("seq", None)
    return jax.shard_map(shards, mesh=mesh, in_specs=in_specs, out_specs=out_specs, check_vma=False)
```

profile of v0, /device:TPU:0, one launch (start us, length us, event | category | flops | bytes accessed | tf_op | source)
XLA Modules:
  0.0 61.2 jit_solution(17865419963159614165)
XLA Ops:
  0.0 0.0 copy-start
  0.0 0.0 copy-start.1
  0.0 5.2 %collective-permute-start = (bf16[1024,512]{1,0:T(8,128)(2,1)}, bf16[1024,512]{1,0:T(8,128)(2,1)S(1)}, u32[]{:S(2)}, u32[]{:S(2)}) collective-permute-start(bf16[1024,512]{1,0:T(8,128)(2,1)} %param.4), channel_id=1, source_target_pairs={{0,2},{1,3},{2,4},{3,5},{4,6},{5,7},{6,8},{7,9},{8,10},{9,11},{10,... | collective-permute-start | bytes 3145736 | tf_op jit(solution)/shard_map/ppermute | solution.py:10
  5.2 2.9 %fusion.6 = f32[1024,1024]{0,1:T(8,128)S(1)} fusion(bf16[1024,512]{1,0:T(8,128)(2,1)} %param.4, bf16[1024,1024]{1,0:T(8,128)(2,1)} %param.6), kind=kOutput, calls=%fused_computation.14 | convolution fusion | flops 1073741824 | bytes 6291456 | tf_op jit(solution)/shard_map/dot_general | solution.py:24
  8.0 0.0 copy-start.2
  8.1 19.8 %collective-permute-done = bf16[1024,512]{1,0:T(8,128)(2,1)S(1)} collective-permute-done((bf16[1024,512]{1,0:T(8,128)(2,1)}, bf16[1024,512]{1,0:T(8,128)(2,1)S(1)}, u32[]{:S(2)}, u32[]{:S(2)}) %collective-permute-start) | collective-permute-done | bytes 1048608 | tf_op jit(solution)/shard_map/ppermute | solution.py:10
  27.8 0.0 copy-done.1
  27.8 1.4 %convolution_add_fusion = f32[1024,1024]{0,1:T(8,128)S(1)} fusion(f32[1024,1024]{0,1:T(8,128)S(1)} %fusion.6, bf16[1024,512]{1,0:T(8,128)(2,1)S(1)} %collective-permute-done, bf16[1024,1024]{1,0:T(8,128)(2,1)S(1)} %copy-done.1), kind=kOutput, calls=%fused_computation | convolution fusion | flops 1074790400 | bytes 10485760 | tf_op jit(solution)/shard_map/dot_general | solution.py:24
  29.2 0.0 copy-done
  29.2 0.0 copy-done.2
  29.2 1.4 %multiply_convert_fusion.1 = (bf16[1024,512]{0,1:T(8,128)(2,1)S(1)}, bf16[1024,512]{0,1:T(8,128)(2,1)S(1)}) fusion(f32[1024,1024]{0,1:T(8,128)S(1)} %convolution_add_fusion, bf16[1024,512]{1,0:T(8,128)(2,1)S(1)} %copy-done.2, bf16[512,512]{1,0:T(8,128)(2,1)S(1)} %copy-done), kind=kOutput, calls=%fused_computation.9 | convolution fusion | flops 543686656 | bytes 7864320 | tf_op jit(solution)/shard_map/dot_general | solution.py:14
  30.7 1.3 %convolution_convert_fusion = bf16[1024,512]{1,0:T(8,128)(2,1)S(1)} fusion(bf16[1024,512]{0,1:T(8,128)(2,1)S(1)} %get-tuple-element.6, bf16[1024,512]{0,1:T(8,128)(2,1)S(1)} %get-tuple-element.5, bf16[1024,1024]{1,0:T(8,128)(2,1)S(1)} %copy-done.1), kind=kOutput, calls=%fused_computation.10 | convolution fusion | flops 1078460416 | bytes 4194304 | tf_op jit(solution)/shard_map/dot_general | solution.py:14
  32.0 1.3 %collective-permute-start.1 = (bf16[1024,512]{1,0:T(8,128)(2,1)S(1)}, bf16[1024,512]{1,0:T(8,128)(2,1)S(1)}, u32[]{:S(2)}, u32[]{:S(2)}) collective-permute-start(bf16[1024,512]{1,0:T(8,128)(2,1)S(1)} %convolution_convert_fusion), channel_id=1, source_target_pairs={{2,0},{3,1},{4,2},{5,3},{6,4},{7,5},{8,6},{9,7},{10,8},{11,9},{12,... | collective-permute-start | bytes 3145736 | tf_op jit(solution)/shard_map/ppermute | solution.py:10
  33.3 25.3 %collective-permute-done.1 = bf16[1024,512]{1,0:T(8,128)(2,1)S(1)} collective-permute-done((bf16[1024,512]{1,0:T(8,128)(2,1)S(1)}, bf16[1024,512]{1,0:T(8,128)(2,1)S(1)}, u32[]{:S(2)}, u32[]{:S(2)}) %collective-permute-start.1) | collective-permute-done | bytes 1048608 | tf_op jit(solution)/shard_map/ppermute | solution.py:10
  58.5 2.6 %convert_add_fusion = f32[1024,512]{1,0:T(8,128)} fusion(bf16[1024,512]{1,0:T(8,128)(2,1)S(1)} %collective-permute-done.1, bf16[1024,512]{1,0:T(8,128)(2,1)S(1)} %copy-done.2, bf16[1024,512]{0,1:T(8,128)(2,1)S(1)} %get-tuple-element.6, bf16[1024,512]{0,1:T(8,128)(2,1)S(1)} %get-tuple-element.5, bf16[1024,1024]{1,0:T(8,128)(2,1)S(1)} %copy-done.1), kind=kOutput, calls=%fused_computation.7 | convolution fusion | flops 1080033280 | bytes 7340032 | tf_op jit(solution)/shard_map/dot_general | solution.py:14
Async XLA Ops:
  0.0 29.2 %copy-start = (bf16[512,512]{1,0:T(8,128)(2,1)S(1)}, bf16[512,512]{1,0:T(8,128)(2,1)}, u32[]{:S(2)}) copy-start(bf16[512,512]{1,0:T(8,128)(2,1)} %param.7) | copy-start | bytes 1572868
  0.0 27.8 %copy-start.1 = (bf16[1024,1024]{1,0:T(8,128)(2,1)S(1)}, bf16[1024,1024]{1,0:T(8,128)(2,1)}, u32[]{:S(2)}) copy-start(bf16[1024,1024]{1,0:T(8,128)(2,1)} %param.6) | copy-start | bytes 6291460
  0.0 27.8 %collective-permute-start = (bf16[1024,512]{1,0:T(8,128)(2,1)}, bf16[1024,512]{1,0:T(8,128)(2,1)S(1)}, u32[]{:S(2)}, u32[]{:S(2)}) collective-permute-start(bf16[1024,512]{1,0:T(8,128)(2,1)} %param.4), channel_id=1, source_target_pairs={{0,2},{1,3},{2,4},{3,5},{4,6},{5,7},{6,8},{7,9},{8,10},{9,11},{10,... | collective-permute-start | bytes 3145736 | tf_op jit(solution)/shard_map/ppermute | solution.py:10
  8.0 21.2 %copy-start.2 = (bf16[1024,512]{1,0:T(8,128)(2,1)S(1)}, bf16[1024,512]{1,0:T(8,128)(2,1)}, u32[]{:S(2)}) copy-start(bf16[1024,512]{1,0:T(8,128)(2,1)} %param.5) | copy-start | bytes 3145732
  32.0 26.6 %collective-permute-start.1 = (bf16[1024,512]{1,0:T(8,128)(2,1)S(1)}, bf16[1024,512]{1,0:T(8,128)(2,1)S(1)}, u32[]{:S(2)}, u32[]{:S(2)}) collective-permute-start(bf16[1024,512]{1,0:T(8,128)(2,1)S(1)} %convolution_convert_fusion), channel_id=1, source_target_pairs={{2,0},{3,1},{4,2},{5,3},{6,4},{7,5},{8,6},{9,7},{10,8},{11,9},{12,... | collective-permute-start | bytes 3145736 | tf_op jit(solution)/shard_map/ppermute | solution.py:10
where the time goes:
time: 62 us; the launch traced here: 61.2 us
  waiting for transfers between devices  45 us (73%)
  matrix products  9.62 us (16%)
  starting transfers between devices  6.45 us (10%)
    ppermute x2, waiting for transfers between devices, from_behind(): return lax.ppermute(block, axis, route)  45 us
    ppermute x2, starting transfers between devices, from_behind(): return lax.ppermute(block, axis, route)  6.45 us
    dot_general x3, matrix products, contract_rows(): lax.dot_general(left, right, (((1,), (1,)), ((), ())), preferred_element_...  5.39 us
    dot_general x1, matrix products, shards(): jnp.dot(signal, w_now, preferred_element_type=jnp.float32)  2.86 us
    dot_general x1, matrix products, shards(): jnp.dot(past, w_past, preferred_element_type=jnp.float32)  1.37 us
  transfers between devices with their start and end apart: 2, of which 2 were waited for; matrix products, arithmetic and copies ran while one was open for 5% of the time, Pallas kernels for 0%

commit v1 on v0

v1 whole, which is shorter than its diff:
```python
import functools

import jax
import jax.numpy as jnp
from jax import lax
from jax.experimental import pallas as pl
from jax.experimental.pallas import tpu as pltpu
from jax.sharding import PartitionSpec as P

MESH = pl.DeviceIdType.MESH
STEPS = 4


def contract_rows(left, right):
    return lax.dot_general(
        left, right, (((1,), (1,)), ((), ())), preferred_element_type=jnp.float32
    )


def kernel(
    devices, steps,
    signal_ref, grad_ref, conv_ref, proj_ref, out_ref,
    feat, grad, grad_home, past, far_in, far_out, sum_in, sum_out, near_b, held,
    conv, proj,
    load_sem, feat_send, feat_recv, grad_send, grad_recv, past_send, past_recv,
    far_send, far_recv, sum_send, sum_recv, store_sem,
):
    me = lax.axis_index("seq")
    odd = lax.rem(lax.div(me, 2), 2)
    partner = me + 2 - 4 * odd
    behind, ahead = me - 4, me + 4
    has_behind, has_ahead = me >= 4, me < devices - 4
    is_odd, is_even = odd == 1, odd == 0
    half, width = feat.shape[1:]
    rows = half // steps
    mine, theirs = odd * half, (1 - odd) * half

    def part(step, base=0):
        return pl.ds(pl.multiple_of(base + step * rows, rows), rows)

    def remote(src, dst, send, recv, target):
        return pltpu.make_async_remote_copy(
            src_ref=src, dst_ref=dst, send_sem=send, recv_sem=recv,
            device_id=(target,), device_id_type=MESH,
        )

    def feat_copy(step, slot):
        return remote(
            signal_ref.at[part(step, theirs)], feat.at[slot, part(step)],
            feat_send.at[step], feat_recv.at[step], partner,
        )

    def grad_copy(step, slot):
        return remote(
            grad_ref.at[part(step, theirs)], grad.at[slot, part(step)],
            grad_send.at[step], grad_recv.at[step], partner,
        )

    def past_copy_own(step):
        return remote(
            signal_ref.at[part(step, mine)], past.at[part(step)],
            past_send.at[step], past_recv.at[step], ahead,
        )

    def past_copy_on(step):
        return remote(
            feat.at[1, part(step)], past.at[part(step)],
            past_send.at[step], past_recv.at[step], ahead,
        )

    def far_copy(step):
        return remote(
            far_out.at[part(step)], far_in.at[part(step)],
            far_send.at[step], far_recv.at[step], behind,
        )

    def sum_copy(step):
        return remote(
            sum_out.at[part(step)], sum_in.at[part(step)],
            sum_send.at[step], sum_recv.at[step], partner,
        )

    def store(step, base, index):
        return pltpu.make_async_copy(
            held.at[part(step, base)], out_ref.at[part(step, base)],
            store_sem.at[index],
        )

    loads = [
        pltpu.make_async_copy(src, dst, load_sem.at[i])
        for i, (src, dst) in enumerate([
            (conv_ref, conv),
            (proj_ref, proj),
            (signal_ref.at[pl.ds(pl.multiple_of(mine, half), half)], feat.at[odd]),
            (grad_ref.at[pl.ds(pl.multiple_of(mine, half), half)], grad.at[odd]),
            (grad_ref.at[pl.ds(pl.multiple_of(theirs, half), half)], grad_home),
        ])
    ]

    barrier = pltpu.get_barrier_semaphore()
    pl.semaphore_signal(barrier, inc=1, device_id=(partner,), device_id_type=MESH)

    @pl.when(has_behind)
    def _():
        pl.semaphore_signal(barrier, inc=1, device_id=(behind,), device_id_type=MESH)

    @pl.when(has_ahead)
    def _():
        pl.semaphore_signal(barrier, inc=1, device_id=(ahead,), device_id_type=MESH)

    for load in loads:
        load.start()
    pl.semaphore_wait(
        barrier, 1 + has_behind.astype(jnp.int32) + has_ahead.astype(jnp.int32)
    )

    for step in range(steps):
        feat_copy(step, odd).start()

        @pl.when(is_odd & has_ahead)
        def _():
            past_copy_own(step).start()

        grad_copy(step, odd).start()

    @pl.when(jnp.logical_not(has_behind))
    def _():
        past[...] = jnp.zeros_like(past)

    @pl.when(jnp.logical_not(has_ahead))
    def _():
        far_in[...] = jnp.zeros_like(far_in)

    for load in loads:
        load.wait()

    def position(before, here, upstream):
        gates = jnp.dot(
            before, conv[:width], preferred_element_type=jnp.float32
        ) + jnp.dot(here, conv[width:], preferred_element_type=jnp.float32)
        tanh_part = jnp.tanh(gates[:, :width])
        sig_part = 0.5 * jnp.tanh(0.5 * gates[:, width:]) + 0.5
        d_mixed = contract_rows(upstream, proj[...])
        scaled = d_mixed * sig_part
        d_tanh = scaled * (1.0 - tanh_part * tanh_part)
        d_sig = scaled * tanh_part * (1.0 - sig_part)
        d_gates = jnp.concatenate(
            [d_tanh.astype(jnp.bfloat16), d_sig.astype(jnp.bfloat16)], 1
        )
        return contract_rows(d_gates, conv[:width]), contract_rows(d_gates, conv[width:])

    def finish(step):
        @pl.when(has_ahead)
        def _():
            far_copy(step).wait_recv()

        total = near_b[part(step)] + far_in[part(step)].astype(jnp.float32)

        @pl.when(is_even)
        def _():
            sum_out[part(step)] = total.astype(jnp.bfloat16)
            sum_copy(step).start()

        @pl.when(is_odd)
        def _():
            held[part(step, mine)] = grad[1, part(step)].astype(jnp.float32) + total
            store(step, mine, step).start()

    def body(step, carry):
        feat_copy(step, 1 - odd).wait_recv()

        @pl.when(is_even & has_ahead)
        def _():
            past_copy_on(step).start()

        @pl.when(is_odd)
        def _():
            grad_copy(step, 1 - odd).wait_recv()

        @pl.when(has_behind)
        def _():
            past_copy_own(step).wait_recv()

        far_a, near_a = position(
            past[part(step)], feat[0, part(step)], grad[0, part(step)]
        )
        far_out[part(step)] = far_a.astype(jnp.bfloat16)

        @pl.when(has_behind)
        def _():
            far_copy(step).start()

        @pl.when(is_even)
        def _():
            grad_copy(step, 1 - odd).wait_recv()

        far_b, nearer = position(
            feat[0, part(step)], feat[1, part(step)], grad[1, part(step)]
        )
        near_b[part(step)] = nearer
        total = near_a + far_b

        @pl.when(is_odd)
        def _():
            sum_out[part(step)] = total.astype(jnp.bfloat16)
            sum_copy(step).start()

        @pl.when(is_even)
        def _():
            held[part(step, mine)] = grad[0, part(step)].astype(jnp.float32) + total
            store(step, mine, step).start()

        @pl.when(step > 0)
        def _():
            finish(step - 1)

        return carry

    lax.fori_loop(0, steps, body, 0)
    finish(steps - 1)

    for step in range(steps):
        sum_copy(step).wait_recv()
        held[part(step, theirs)] = grad_home[part(step)].astype(jnp.float32) + sum_in[
            part(step)
        ].astype(jnp.float32)
        store(step, theirs, steps + step).start()

    for step in range(steps):
        feat_copy(step, odd).wait_send()
        grad_copy(step, odd).wait_send()
        sum_copy(step).wait_send()

        @pl.when(has_ahead)
        def _():
            past_copy_own(step).wait_send()

        @pl.when(has_behind)
        def _():
            far_copy(step).wait_send()

        store(step, mine, step).wait()
        store(step, theirs, steps + step).wait()


def shards(signal, grad_out, conv_weight, proj_weight):
    devices = lax.axis_size("seq")
    count, width = signal.shape
    half = count // 2
    narrow = pltpu.VMEM((half, width), jnp.bfloat16)
    pair = pltpu.VMEM((2, half, width), jnp.bfloat16)
    per_step = pltpu.SemaphoreType.DMA((STEPS,))
    return pl.pallas_call(
        functools.partial(kernel, devices, STEPS),
        out_shape=jax.ShapeDtypeStruct((count, width), jnp.float32),
        in_specs=[pl.BlockSpec(memory_space=pl.ANY)] * 4,
        out_specs=pl.BlockSpec(memory_space=pl.ANY),
        scratch_shapes=[
            pair, pair, narrow, narrow, narrow, narrow, narrow, narrow,
            pltpu.VMEM((half, width), jnp.float32),
            pltpu.VMEM((count, width), jnp.float32),
            pltpu.VMEM(conv_weight.shape, jnp.bfloat16),
            pltpu.VMEM(proj_weight.shape, jnp.bfloat16),
            pltpu.SemaphoreType.DMA((5,)),
        ] + [per_step] * 10 + [pltpu.SemaphoreType.DMA((2 * STEPS,))],
        compiler_params=pltpu.CompilerParams(
            collective_id=0, has_side_effects=True, vmem_limit_bytes=48 * 2**20
        ),
        cost_estimate=pl.CostEstimate(
            flops=2 * count * width * width * 9,
            bytes_accessed=16 * count * width,
            transcendentals=2 * count * width,
        ),
    )(signal, grad_out, conv_weight, proj_weight)


def solution(mesh):
    in_specs = (P("seq", None), P("seq", None), P(), P())
    out_specs = P("seq", None)
    return jax.shard_map(shards, mesh=mesh, in_specs=in_specs, out_specs=out_specs, check_vma=False)
```

time: 62 us -> 51.7 us (0.83)
  the two profiles are of different devices: /device:TPU:0 before, /device:TPU:10 now
where the time goes in v1:
time: 51.7 us; the launch traced here: 51.5 us
  Pallas kernels  46.7 us (90%)
  local copies, waits for them, and re-layouts  4.81 us (9%)
    pallas_call x1, Pallas kernels, shards(): pl.pallas_call(functools.partial(kernel, devices, STEPS), out_shape=jax.S...  46.7 us
    unnamed x7, local copies, waits for them, and re-layouts  4.81 us

profile of v1, /device:TPU:10, one launch (start us, length us, event | category | flops | bytes accessed | tf_op | source)
XLA Modules:
  0.0 51.5 jit_solution(3811535987078101477)
XLA Ops:
  0.0 0.0 copy-start
  0.0 1.2 %copy-done = bf16[1024,512]{1,0:T(8,128)(2,1)S(1)} copy-done((bf16[1024,512]{1,0:T(8,128)(2,1)S(1)}, bf16[1024,512]{1,0:T(8,128)(2,1)}, u32[]{:S(2)}) %copy-start) | copy-done | bytes 1048600
  1.2 0.0 copy-start.1
  1.2 1.2 %copy-done.1 = bf16[1024,512]{1,0:T(8,128)(2,1)S(1)} copy-done((bf16[1024,512]{1,0:T(8,128)(2,1)S(1)}, bf16[1024,512]{1,0:T(8,128)(2,1)}, u32[]{:S(2)}) %copy-start.1) | copy-done | bytes 1048600
  2.5 0.0 copy-start.2
  2.5 1.0 %copy-done.2 = bf16[512,512]{1,0:T(8,128)(2,1)S(1)} copy-done((bf16[512,512]{1,0:T(8,128)(2,1)S(1)}, bf16[512,512]{1,0:T(8,128)(2,1)}, u32[]{:S(2)}) %copy-start.2) | copy-done | bytes 524312
  3.5 46.7 %shard_map.46 = f32[1024,512]{1,0:T(8,128)S(1)} custom-call(bf16[1024,512]{1,0:T(8,128)(2,1)S(1)} %copy-done, bf16[1024,512]{1,0:T(8,128)(2,1)S(1)} %copy-done.1, bf16[1024,1024]{1,0:T(8,128)(2,1)} %conv_ref.1, bf16[512,512]{1,0:T(8,128)(2,1)S(1)} %copy-done.2), custom_call_target="tpu_custom_call" | custom-call | flops 4831838208 | bytes 8388608 | tf_op jit(solution)/shard_map/pallas_call | solution.py:253
  50.2 1.3 %copy.6 = f32[1024,512]{1,0:T(8,128)} copy(f32[1024,512]{1,0:T(8,128)S(1)} %shard_map.46) | data formatting | bytes 4194304
Async XLA Ops:
  0.0 1.2 %copy-start = (bf16[1024,512]{1,0:T(8,128)(2,1)S(1)}, bf16[1024,512]{1,0:T(8,128)(2,1)}, u32[]{:S(2)}) copy-start(bf16[1024,512]{1,0:T(8,128)(2,1)} %signal_ref.1) | copy-start | bytes 3145732
  1.2 1.2 %copy-start.1 = (bf16[1024,512]{1,0:T(8,128)(2,1)S(1)}, bf16[1024,512]{1,0:T(8,128)(2,1)}, u32[]{:S(2)}) copy-start(bf16[1024,512]{1,0:T(8,128)(2,1)} %grad_ref.1) | copy-start | bytes 3145732
  2.5 1.0 %copy-start.2 = (bf16[512,512]{1,0:T(8,128)(2,1)S(1)}, bf16[512,512]{1,0:T(8,128)(2,1)}, u32[]{:S(2)}) copy-start(bf16[512,512]{1,0:T(8,128)(2,1)} %proj_ref.1) | copy-start | bytes 1572868

commit v2 on v1

--- a/solution.py
+++ b/solution.py
@@ -20,7 +20,7 @@
 def kernel(
     devices, steps,
     signal_ref, grad_ref, conv_ref, proj_ref, out_ref,
-    feat, grad, grad_home, past, far_in, far_out, sum_in, sum_out, near_b, held,
+    chain, grad, grad_home, far_in, far_out, sum_in, sum_out, near_b, held,
     conv, proj,
     load_sem, feat_send, feat_recv, grad_send, grad_recv, past_send, past_recv,
     far_send, far_recv, sum_send, sum_recv, store_sem,
@@ -31,7 +31,7 @@
     behind, ahead = me - 4, me + 4
     has_behind, has_ahead = me >= 4, me < devices - 4
     is_odd, is_even = odd == 1, odd == 0
-    half, width = feat.shape[1:]
+    half, width = grad.shape[1:]
     rows = half // steps
     mine, theirs = odd * half, (1 - odd) * half
 
@@ -46,7 +46,7 @@
 
     def feat_copy(step, slot):
         return remote(
-            signal_ref.at[part(step, theirs)], feat.at[slot, part(step)],
+            signal_ref.at[part(step, theirs)], chain.at[1 + slot, part(step)],
             feat_send.at[step], feat_recv.at[step], partner,
         )
 
@@ -58,13 +58,13 @@
 
     def past_copy_own(step):
         return remote(
-            signal_ref.at[part(step, mine)], past.at[part(step)],
+            signal_ref.at[part(step, mine)], chain.at[0, part(step)],
             past_send.at[step], past_recv.at[step], ahead,
         )
 
     def past_copy_on(step):
         return remote(
-            feat.at[1, part(step)], past.at[part(step)],
+            chain.at[2, part(step)], chain.at[0, part(step)],
             past_send.at[step], past_recv.at[step], ahead,
         )
 
@@ -91,7 +91,7 @@
         for i, (src, dst) in enumerate([
             (conv_ref, conv),
             (proj_ref, proj),
-            (signal_ref.at[pl.ds(pl.multiple_of(mine, half), half)], feat.at[odd]),
+            (signal_ref.at[pl.ds(pl.multiple_of(mine, half), half)], chain.at[1 + odd]),
             (grad_ref.at[pl.ds(pl.multiple_of(mine, half), half)], grad.at[odd]),
             (grad_ref.at[pl.ds(pl.multiple_of(theirs, half), half)], grad_home),
         ])
@@ -125,7 +125,7 @@
 
     @pl.when(jnp.logical_not(has_behind))
     def _():
-        past[...] = jnp.zeros_like(past)
+        chain[0] = jnp.zeros((half, width), chain.dtype)
 
     @pl.when(jnp.logical_not(has_ahead))
     def _():
@@ -134,7 +134,7 @@
     for load in loads:
         load.wait()
 
-    def position(before, here, upstream):
+    def positions(before, here, upstream):
         gates = jnp.dot(
             before, conv[:width], preferred_element_type=jnp.float32
         ) + jnp.dot(here, conv[width:], preferred_element_type=jnp.float32)
@@ -159,65 +159,76 @@
         @pl.when(is_even)
         def _():
             sum_out[part(step)] = total.astype(jnp.bfloat16)
-            sum_copy(step).start()
 
         @pl.when(is_odd)
         def _():
             held[part(step, mine)] = grad[1, part(step)].astype(jnp.float32) + total
             store(step, mine, step).start()
 
+    def pass_on(step):
+        feat_copy(step, 1 - odd).wait_recv()
+
+        @pl.when(is_even & has_ahead)
+        def _():
+            past_copy_on(step).start()
+
+    pass_on(0)
+
     def body(step, carry):
-        feat_copy(step, 1 - odd).wait_recv()
-
-        @pl.when(is_even & has_ahead)
-        def _():
-            past_copy_on(step).start()
+        @pl.when(step + 1 < steps)
+        def _():
+            pass_on(step + 1)
+
+        grad_copy(step, 1 - odd).wait_recv()
+
+        @pl.when(step > 1)
+        def _():
+            finish(step - 2)
+            sum_copy(step - 2).start()
+
+
+        @pl.when(has_behind)
+        def _():
+            past_copy_own(step).wait_recv()
+
+        flat = (2 * rows, width)
+        far, near = positions(
+            chain[0:2, part(step)].reshape(flat),
+            chain[1:3, part(step)].reshape(flat),
+            grad[:, part(step)].reshape(flat),
+        )
+        far_out[part(step)] = far[:rows].astype(jnp.bfloat16)
+
+        @pl.when(has_behind)
+        def _():
+            far_copy(step).start()
+
+        near_b[part(step)] = near[rows:]
+        total = near[:rows] + far[rows:]
 
         @pl.when(is_odd)
         def _():
-            grad_copy(step, 1 - odd).wait_recv()
-
-        @pl.when(has_behind)
-        def _():
-            past_copy_own(step).wait_recv()
-
-        far_a, near_a = position(
-            past[part(step)], feat[0, part(step)], grad[0, part(step)]
-        )
-        far_out[part(step)] = far_a.astype(jnp.bfloat16)
-
-        @pl.when(has_behind)
-        def _():
-            far_copy(step).start()
-
-        @pl.when(is_even)
-        def _():
-            grad_copy(step, 1 - odd).wait_recv()
-
-        far_b, nearer = position(
-            feat[0, part(step)], feat[1, part(step)], grad[1, part(step)]
-        )
-        near_b[part(step)] = nearer
-        total = near_a + far_b
-
-        @pl.when(is_odd)
-        def _():
             sum_out[part(step)] = total.astype(jnp.bfloat16)
-            sum_copy(step).start()
 
         @pl.when(is_even)
         def _():
             held[part(step, mine)] = grad[0, part(step)].astype(jnp.float32) + total
             store(step, mine, step).start()
 
-        @pl.when(step > 0)
-        def _():
-            finish(step - 1)
-
         return carry
 
     lax.fori_loop(0, steps, body, 0)
-    finish(steps - 1)
+
+    for step in range(steps - 2, steps):
+        @pl.when(is_odd)
+        def _():
+            sum_copy(step).start()
+
+        finish(step)
+
+        @pl.when(is_even)
+        def _():
+            sum_copy(step).start()
 
     for step in range(steps):
         sum_copy(step).wait_recv()
@@ -256,7 +267,8 @@
         in_specs=[pl.BlockSpec(memory_space=pl.ANY)] * 4,
         out_specs=pl.BlockSpec(memory_space=pl.ANY),
         scratch_shapes=[
-            pair, pair, narrow, narrow, narrow, narrow, narrow, narrow,
+            pltpu.VMEM((3, half, width), jnp.bfloat16),
+            pair, narrow, narrow, narrow, narrow, narrow,
             pltpu.VMEM((half, width), jnp.float32),
             pltpu.VMEM((count, width), jnp.float32),
             pltpu.VMEM(conv_weight.shape, jnp.bfloat16),
@@ -264,7 +276,7 @@
             pltpu.SemaphoreType.DMA((5,)),
         ] + [per_step] * 10 + [pltpu.SemaphoreType.DMA((2 * STEPS,))],
         compiler_params=pltpu.CompilerParams(
-            collective_id=0, has_side_effects=True, vmem_limit_bytes=48 * 2**20
+            collective_id=0, has_side_effects=True, vmem_limit_bytes=60 * 2**20
         ),
         cost_estimate=pl.CostEstimate(
             flops=2 * count * width * width * 9,

time: 51.7 us -> 43.2 us (0.84)
  the two profiles are of different devices: /device:TPU:10 before, /device:TPU:0 now
where the time goes in v2:
time: 43.2 us; the launch traced here: 43.1 us
  Pallas kernels  40 us (93%)
  local copies, waits for them, and re-layouts  3.08 us (7%)
    pallas_call x1, Pallas kernels, shards(): pl.pallas_call(functools.partial(kernel, devices, STEPS), out_shape=jax.S...  40 us
    unnamed x1, local copies, waits for them, and re-layouts  3.08 us

profile of v2, /device:TPU:0, one launch (start us, length us, event | category | flops | bytes accessed | tf_op | source)
XLA Modules:
  0.0 43.1 jit_solution(14625144947548948952)
XLA Ops:
  0.0 40.0 %shard_map.46 = f32[1024,512]{1,0:T(8,128)} custom-call(bf16[1024,512]{1,0:T(8,128)(2,1)} %signal_ref.1, bf16[1024,512]{1,0:T(8,128)(2,1)} %grad_ref.1, bf16[1024,1024]{1,0:T(8,128)(2,1)} %conv_ref.1, bf16[512,512]{1,0:T(8,128)(2,1)} %proj_ref.1), custom_call_target="tpu_custom_call" | custom-call | flops 4831838208 | bytes 8388608 | tf_op jit(solution)/shard_map/pallas_call | solution.py:264
  40.0 3.1 %copy.6 = f32[1024,512]{1,0:T(8,128)} copy(f32[1024,512]{1,0:T(8,128)} %shard_map.46) | data formatting | bytes 4194304

commit v3 on v2

--- a/solution.py
+++ b/solution.py
@@ -20,10 +20,10 @@
 def kernel(
     devices, steps,
     signal_ref, grad_ref, conv_ref, proj_ref, out_ref,
-    chain, grad, grad_home, far_in, far_out, sum_in, sum_out, near_b, held,
+    chain, grad, grad_home, far_in, far_out, sum_in, sum_out, near_b,
     conv, proj,
     load_sem, feat_send, feat_recv, grad_send, grad_recv, past_send, past_recv,
-    far_send, far_recv, sum_send, sum_recv, store_sem,
+    far_send, far_recv, sum_send, sum_recv,
 ):
     me = lax.axis_index("seq")
     odd = lax.rem(lax.div(me, 2), 2)
@@ -78,12 +78,6 @@
         return remote(
             sum_out.at[part(step)], sum_in.at[part(step)],
             sum_send.at[step], sum_recv.at[step], partner,
-        )
-
-    def store(step, base, index):
-        return pltpu.make_async_copy(
-            held.at[part(step, base)], out_ref.at[part(step, base)],
-            store_sem.at[index],
         )
 
     loads = [
@@ -162,8 +156,7 @@
 
         @pl.when(is_odd)
         def _():
-            held[part(step, mine)] = grad[1, part(step)].astype(jnp.float32) + total
-            store(step, mine, step).start()
+            out_ref[part(step, mine)] = grad[1, part(step)].astype(jnp.float32) + total
 
     def pass_on(step):
         feat_copy(step, 1 - odd).wait_recv()
@@ -212,8 +205,7 @@
 
         @pl.when(is_even)
         def _():
-            held[part(step, mine)] = grad[0, part(step)].astype(jnp.float32) + total
-            store(step, mine, step).start()
+            out_ref[part(step, mine)] = grad[0, part(step)].astype(jnp.float32) + total
 
         return carry
 
@@ -232,10 +224,9 @@
 
     for step in range(steps):
         sum_copy(step).wait_recv()
-        held[part(step, theirs)] = grad_home[part(step)].astype(jnp.float32) + sum_in[
+        out_ref[part(step, theirs)] = grad_home[part(step)].astype(jnp.float32) + sum_in[
             part(step)
         ].astype(jnp.float32)
-        store(step, theirs, steps + step).start()
 
     for step in range(steps):
         feat_copy(step, odd).wait_send()
@@ -249,9 +240,6 @@
         @pl.when(has_behind)
         def _():
             far_copy(step).wait_send()
-
-        store(step, mine, step).wait()
-        store(step, theirs, steps + step).wait()
 
 
 def shards(signal, grad_out, conv_weight, proj_weight):
@@ -263,18 +251,17 @@
     per_step = pltpu.SemaphoreType.DMA((STEPS,))
     return pl.pallas_call(
         functools.partial(kernel, devices, STEPS),
-        out_shape=jax.ShapeDtypeStruct((count, width), jnp.float32),
+        out_shape=pltpu.VMEM((count, width), jnp.float32),
         in_specs=[pl.BlockSpec(memory_space=pl.ANY)] * 4,
-        out_specs=pl.BlockSpec(memory_space=pl.ANY),
+        out_specs=pl.BlockSpec(memory_space=pltpu.VMEM),
         scratch_shapes=[
             pltpu.VMEM((3, half, width), jnp.bfloat16),
             pair, narrow, narrow, narrow, narrow, narrow,
             pltpu.VMEM((half, width), jnp.float32),
-            pltpu.VMEM((count, width), jnp.float32),
             pltpu.VMEM(conv_weight.shape, jnp.bfloat16),
             pltpu.VMEM(proj_weight.shape, jnp.bfloat16),
             pltpu.SemaphoreType.DMA((5,)),
-        ] + [per_step] * 10 + [pltpu.SemaphoreType.DMA((2 * STEPS,))],
+        ] + [per_step] * 10,
         compiler_params=pltpu.CompilerParams(
             collective_id=0, has_side_effects=True, vmem_limit_bytes=60 * 2**20
         ),

time: 43.2 us -> 40.7 us (0.942)
  local copies, waits for them, and re-layouts: 3.08 us -> 1.32 us
  Pallas kernels: 40 us -> 39.2 us
    unnamed x1, local copies, waits for them, and re-layouts: 3.08 us -> 1.32 us
    pallas_call x1, Pallas kernels: 40 us -> 39.2 us  [shards(): pl.pallas_call(functools.partial(kernel, devices, STEPS), out_shape=pltpu...]
where the time goes in v3:
time: 40.7 us; the launch traced here: 40.6 us
  Pallas kernels  39.2 us (96%)
  local copies, waits for them, and re-layouts  1.32 us (3%)
    pallas_call x1, Pallas kernels, shards(): pl.pallas_call(functools.partial(kernel, devices, STEPS), out_shape=pltpu...  39.2 us
    unnamed x1, local copies, waits for them, and re-layouts  1.32 us

profile of v3, /device:TPU:0, one launch (start us, length us, event | category | flops | bytes accessed | tf_op | source)
XLA Modules:
  0.0 40.6 jit_solution(18143158464731322138)
XLA Ops:
  0.0 39.2 %shard_map.46 = f32[1024,512]{1,0:T(8,128)S(1)} custom-call(bf16[1024,512]{1,0:T(8,128)(2,1)} %signal_ref.1, bf16[1024,512]{1,0:T(8,128)(2,1)} %grad_ref.1, bf16[1024,1024]{1,0:T(8,128)(2,1)} %conv_ref.1, bf16[512,512]{1,0:T(8,128)(2,1)} %proj_ref.1), custom_call_target="tpu_custom_call" | custom-call | flops 4831838208 | bytes 8388608 | tf_op jit(solution)/shard_map/pallas_call | solution.py:252
  39.2 1.3 %copy.6 = f32[1024,512]{1,0:T(8,128)} copy(f32[1024,512]{1,0:T(8,128)S(1)} %shard_map.46) | data formatting | bytes 4194304

commit v4 on v3

--- a/solution.py
+++ b/solution.py
@@ -174,48 +174,48 @@
 
         grad_copy(step, 1 - odd).wait_recv()
 
-        @pl.when(step > 1)
-        def _():
-            finish(step - 2)
-            sum_copy(step - 2).start()
-
 
         @pl.when(has_behind)
         def _():
             past_copy_own(step).wait_recv()
 
-        flat = (2 * rows, width)
-        far, near = positions(
-            chain[0:2, part(step)].reshape(flat),
-            chain[1:3, part(step)].reshape(flat),
-            grad[:, part(step)].reshape(flat),
-        )
-        far_out[part(step)] = far[:rows].astype(jnp.bfloat16)
+        far_a, near_a = positions(
+            chain[0, part(step)], chain[1, part(step)], grad[0, part(step)]
+        )
+        far_out[part(step)] = far_a.astype(jnp.bfloat16)
 
         @pl.when(has_behind)
         def _():
             far_copy(step).start()
 
-        near_b[part(step)] = near[rows:]
-        total = near[:rows] + far[rows:]
+        far_b, nearer = positions(
+            chain[1, part(step)], chain[2, part(step)], grad[1, part(step)]
+        )
+        near_b[part(step)] = nearer
+        total = near_a + far_b
 
         @pl.when(is_odd)
         def _():
             sum_out[part(step)] = total.astype(jnp.bfloat16)
+            sum_copy(step).start()
 
         @pl.when(is_even)
         def _():
             out_ref[part(step, mine)] = grad[0, part(step)].astype(jnp.float32) + total
 
+        @pl.when(step > 0)
+        def _():
+            finish(step - 1)
+
+            @pl.when(is_even)
+            def _():
+                sum_copy(step - 1).start()
+
         return carry
 
     lax.fori_loop(0, steps, body, 0)
 
-    for step in range(steps - 2, steps):
-        @pl.when(is_odd)
-        def _():
-            sum_copy(step).start()
-
+    for step in range(steps - 1, steps):
         finish(step)
 
         @pl.when(is_even)

time: 40.7 us -> 40.7 us (level)
  no operation moved by 1% of the time
where the time goes in v4:
time: 40.7 us; the launch traced here: 40.6 us
  Pallas kernels  39.2 us (96%)
  local copies, waits for them, and re-layouts  1.32 us (3%)
    pallas_call x1, Pallas kernels, shards(): pl.pallas_call(functools.partial(kernel, devices, STEPS), out_shape=pltpu...  39.2 us
    unnamed x1, local copies, waits for them, and re-layouts  1.32 us

profile of v4, /device:TPU:0, one launch (start us, length us, event | category | flops | bytes accessed | tf_op | source)
XLA Modules:
  0.0 40.6 jit_solution(10857104403900878578)
XLA Ops:
  0.0 39.2 %shard_map.46 = f32[1024,512]{1,0:T(8,128)S(1)} custom-call(bf16[1024,512]{1,0:T(8,128)(2,1)} %signal_ref.1, bf16[1024,512]{1,0:T(8,128)(2,1)} %grad_ref.1, bf16[1024,1024]{1,0:T(8,128)(2,1)} %conv_ref.1, bf16[512,512]{1,0:T(8,128)(2,1)} %proj_ref.1), custom_call_target="tpu_custom_call" | custom-call | flops 4831838208 | bytes 8388608 | tf_op jit(solution)/shard_map/pallas_call | solution.py:252
  39.2 1.3 %copy.6 = f32[1024,512]{1,0:T(8,128)} copy(f32[1024,512]{1,0:T(8,128)S(1)} %shard_map.46) | data formatting | bytes 4194304
